TPU v7x, 32 devices: a whole 2x2x4 slice. The times are simulated.
32 devices in a mesh: groups: 2 (over x), ctx: 4 (over y, core), head: 4 (over z).
Axes of the slice: x: 2, y: 2, z: 4, core: 2. Of those that a mesh axis runs over, the one named last changes fastest.
Arguments:
- xs: bfloat16 [12288, 4096], P(('groups', 'ctx', 'head')), parts along dimension 0, may hold values from -6 to 6
- gate_in: bfloat16 [12288, 4096], P(('groups', 'ctx', 'head')), parts along dimension 0, may hold values from -6 to 6
- bc: bfloat16 [12288, 256], P(('groups', 'ctx', 'head')), parts along dimension 0, may hold values from -1.78125 to 1.78125
- dt_raw: bfloat16 [12288, 64], P(('groups', 'ctx', 'head')), parts along dimension 0, may hold values from -4 to 4
- doc_ids: int32 [12288], P(('groups', 'ctx')), parts along dimension 0, may hold values from 0 to 31, never falling along the last dimension, each value on 1 to 3072 neighbouring positions
- dt_bias: float32 [64], P('head'), may hold values from -1 to 1
- decay_rate: float32 [64], P('head'), may hold values from 8.138021e-06 to 0.03
- skip: float32 [64], P('head'), may hold values from 0.5 to 1.5
- norm_gain: float32 [4096], replicated, may hold values from 0.5 to 1.5
Outputs:
- mixed: bfloat16 [12288, 4096], P(('groups', 'ctx', 'head')), parts along dimension 0
There are 2 independent parts, one for each index of `groups`. A program takes and returns all parts, laid end to end along the dimension named above; an argument that names none is the same for every part. Nothing has to cross between parts.
Inputs may be any that keep to these rules, and one draw needn't show every extreme that they name: `doc_ids`: document ids never fall along the window; each document is one run of tokens, at most 3072 long, and one document is exactly that long.
All inputs are finite; a program needn't handle non-finite values.
Results may differ from a plain program's by a relative error of at most 0.007.
Values may be sent and summed in bfloat16 or wider, within the bound.
A program may use at most 64 MiB of HBM per device.

v0:
```python
import jax
import jax.numpy as jnp
from jax import lax
from jax.sharding import PartitionSpec as P

STATE = 128
EXTRA = 16
SPAN_AXES = ("ctx", "head")


def shards(xs, gate_in, bc, dt_raw, doc_ids, dt_bias, decay_rate, skip, norm_gain):
    f32, bf16 = (jnp.float32, jnp.bfloat16)
    tokens, columns = xs.shape
    heads = dt_raw.shape[1]
    hdim = columns // heads
    devices = lax.axis_size("ctx") * lax.axis_size("head")
    own = columns // devices
    params = lax.all_gather(jnp.stack([dt_bias, decay_rate, skip]), "head", axis=1, tiled=True)
    ids = lax.dynamic_slice(doc_ids, (lax.axis_index("head") * tokens,), (tokens,))
    dt = jax.nn.softplus(dt_raw.astype(f32) + params[0][None, :])
    lower = jnp.arange(tokens)[:, None] >= jnp.arange(tokens)[None, :]
    log_decay = -jnp.dot(
        lower.astype(f32), dt * params[1][None, :], precision=lax.Precision.HIGHEST
    )
    log_end = log_decay[-1]
    middle = 0.5 * log_end
    spread = lambda v: jnp.repeat(v, hdim, axis=-1)
    into = jnp.exp(middle[None, :] - log_decay) * dt
    out_of = jnp.exp(log_decay - middle[None, :])
    x = xs.astype(f32)
    weighted = (spread(into) * x).astype(bf16)
    in_b, in_c = (bc[:, :STATE], bc[:, STATE:])
    scores = jnp.einsum("tn,sn->ts", in_c, in_b, preferred_element_type=f32)
    scores = jnp.where(lower & (ids[:, None] == ids[None, :]), scores, 0.0).astype(bf16)
    last_b = jnp.where((ids == ids[-1])[:, None], in_b, jnp.zeros_like(in_b))
    state = jnp.einsum("sn,sq->nq", last_b, weighted, preferred_element_type=f32)
    state = (state * spread(jnp.exp(middle))[None, :]).astype(bf16)
    factor = spread(jnp.exp(log_end))
    factor_hi = factor.astype(bf16)
    factor_lo = (factor - factor_hi.astype(f32)).astype(bf16)
    back = jnp.full((columns,), ids[-1].astype(bf16))
    extra = jnp.concatenate(
        [jnp.stack([factor_hi, factor_lo, back]), jnp.zeros((EXTRA - 3, columns), bf16)]
    )
    block = jnp.concatenate([state, extra])
    block = block.reshape(STATE + EXTRA, devices, own).transpose(1, 0, 2)
    got = lax.all_to_all(block, SPAN_AXES, split_axis=0, concat_axis=0, tiled=True)

    def advance(carry, piece):
        entering, before = carry
        mult = piece[STATE].astype(f32) + piece[STATE + 1].astype(f32)
        back_id = piece[STATE + 2].astype(f32)
        give = jnp.concatenate(
            [entering.astype(bf16), before[None].astype(bf16), jnp.zeros((EXTRA - 1, own), bf16)]
        )
        keep = jnp.where(back_id == before, mult, 0.0)
        return ((keep[None] * entering + piece[:STATE].astype(f32), back_id), give)

    unused, give = lax.scan(
        advance, (jnp.zeros((STATE, own), f32), jnp.full((own,), -1.0, f32)), got
    )
    back_here = lax.all_to_all(give, SPAN_AXES, split_axis=0, concat_axis=0, tiled=True)
    back_here = back_here.transpose(1, 0, 2).reshape(STATE + EXTRA, columns)
    before = back_here[STATE, 0].astype(f32)
    inside_c = jnp.where((ids.astype(f32) == before)[:, None], in_c, jnp.zeros_like(in_c))
    carried = jnp.dot(inside_c, back_here[:STATE], preferred_element_type=f32)
    local = jnp.dot(scores, weighted, preferred_element_type=f32)
    ssm = (
        spread(out_of) * (local + carried * spread(jnp.exp(middle))[None, :])
        + spread(params[2])[None, :] * x
    )
    gated = ssm.astype(bf16).astype(f32) * jax.nn.silu(gate_in.astype(f32))
    scale = lax.rsqrt(jnp.mean(gated * gated, axis=-1, keepdims=True) + 1e-05)
    return (gated * scale * norm_gain[None, :]).astype(bf16)


def solution(mesh):
    rows = P(("groups", "ctx", "head"), None)
    return jax.shard_map(
        shards,
        mesh=mesh,
        in_specs=(
            rows,
            rows,
            rows,
            rows,
            P(("groups", "ctx")),
            P("head"),
            P("head"),
            P("head"),
            P(),
        ),
        out_specs=rows,
        check_vma=False,
    )
```

profile of v0, /device:TPU:0, one launch (start us, length us, event | category | flops | bytes accessed | tf_op | source)
XLA Modules:
  0.0 152.1 jit_solution(1938761750910926963)
XLA Ops:
  0.0 0.8 dynamic_slice.7
  0.8 0.6 slice.52
  1.4 1.4 broadcast_compare_fusion
  3.4 0.7 maximum_bitcast_fusion.1
  4.1 13.5 %all-gather = f32[4,16,3]{1,2,0:T(4,128)S(1)} all-gather(f32[1,16,3]{1,2,0:T(4,128)S(1)} %maximum_bitcast_fusion.1), channel_id=1, replica_groups=mesh['groups'=2,'ctx'=4,'head'=4] {'head'}, dimensions={0}, use_global_device_ids=true | all-gather | bytes 960 | tf_op jit(solution)/shard_map/all_gather | solution.py:18
  17.7 0.1 reshape.110
  17.8 1.3 convolution_negate_fusion
  19.0 0.2 exponential_reduce_fusion
  19.3 0.9 exponential_multiply_fusion
  20.4 3.1 %broadcast_in_dim.69 = f32[384,64,64]{0,2,1:T(8,128)} broadcast(f32[384,64]{0,1:T(8,128)S(1)} %get-tuple-element.66), dimensions={0,1} | broadcast | bytes 6389760 | tf_op jit(solution)/shard_map/broadcast_in_dim | solution.py:27
  23.4 6.8 %copy.20 = f32[384,4096]{1,0:T(8,128)} copy(f32[384,4096]{0,1:T(8,128)} %bitcast.51) | data formatting | bytes 12582912 | tf_op jit(solution)/shard_map/reshape | solution.py:27
  30.2 3.7 %fusion.12 = bf16[128,4096]{1,0:T(8,128)(2,1)S(1)} fusion(f32[4096]{0:T(1024)S(1)} %mul.100, pred[384]{0:T(512)(128)(4,1)S(1)} %broadcast_compare_fusion, bf16[384,256]{1,0:T(8,128)(2,1)S(1)} %copy-done.1, f32[384,4096]{1,0:T(8,128)} %copy.20, bf16[384,4096]{1,0:T(8,128)(2,1)S(1)} %copy-done), kind=kOutput, calls=%fused_computation.27 | convolution fusion | flops 408469504 | bytes 10600960 | tf_op jit(solution)/shard_map/sn,sq->nq/dot_general | solution.py:36
  33.9 0.1 copy.29
  34.0 0.1 exp.34
  34.1 0.1 broadcast_in_dim.75
  34.2 0.1 broadcast_in_dim.76
  34.4 5.4 %concatenate.10 = bf16[144,16,256]{2,0,1:T(8,128)(2,1)} concatenate(bf16[128,16,256]{2,0,1:T(8,128)(2,1)S(1)} %bitcast.55, bf16[1,16,256]{2,0,1:T(2,128)(2,1)S(1)} %get-tuple-element.69, bf16[1,16,256]{2,0,1:T(2,128)(2,1)S(1)} %get-tuple-element.68, bf16[1,16,256]{2,0,1:T(2,128)(2,1)S(1)} %stack_broadcast_in_dim.3, bf16[13,16,256]{2,0,1:T(8,128)(2,1)S(1)} %broadcast_in_dim.77), dimensions={0} | concatenate | bytes 2359296 | tf_op jit(solution)/shard_map/concatenate | solution.py:45
  39.8 4.5 %all-to-all-start = ((bf16[16,144,256]{2,1,0:T(8,128)(2,1)}), bf16[16,144,256]{2,1,0:T(8,128)(2,1)S(1)}, u32[]{:S(2)}, u32[]{:S(2)}) async-start(bf16[16,144,256]{2,1,0:T(8,128)(2,1)} %bitcast.11), calls=%async_computation | async-start | bytes 2359296 | tf_op jit(solution)/shard_map/all_to_all | solution.py:47
  44.2 29.8 %all-to-all-done = bf16[16,144,256]{2,1,0:T(8,128)(2,1)S(1)} async-done(((bf16[16,144,256]{2,1,0:T(8,128)(2,1)}), bf16[16,144,256]{2,1,0:T(8,128)(2,1)S(1)}, u32[]{:S(2)}, u32[]{:S(2)}) %all-to-all-start) | async-done | bytes 1179680 | tf_op jit(solution)/shard_map/all_to_all | solution.py:47
  74.0 15.2 %while.15 = (s32[]{:T(128)}, f32[128,256]{1,0:T(8,128)S(1)}, f32[256]{0:T(256)S(1)}, bf16[16,144,256]{2,1,0:T(8,128)(2,1)}, bf16[16,144,256]{2,1,0:T(8,128)(2,1)...) while((s32[]{:T(128)}, f32[128,256]{1,0:T(8,128)S(1)}, ...), condition=%wide.region_1.2_spmd.clone, body=%wide.region_0.1_spmd.clone.sunk | while | flops 386822 | bytes 677192 | solution.py:59
  74.2 0.7 fusion.57
  75.2 0.7 fusion.57
  76.1 0.7 fusion.57
  77.1 0.7 fusion.57
  78.0 0.7 fusion.57
  79.0 0.7 fusion.57
  79.9 0.7 fusion.57
  80.9 0.7 fusion.57
  81.9 0.7 fusion.57
  82.8 0.7 fusion.57
  83.8 0.7 fusion.57
  84.7 0.7 fusion.57
  85.7 0.7 fusion.57
  86.6 0.7 fusion.57
  87.6 0.7 fusion.57
  88.5 0.7 fusion.57
  89.2 3.7 %all-to-all-start.1 = ((bf16[16,144,256]{2,1,0:T(8,128)(2,1)}), bf16[16,144,256]{2,1,0:T(8,128)(2,1)S(1)}, u32[]{:S(2)}, u32[]{:S(2)}) async-start(bf16[16,144,256]{2,1,0:T(8,128)(2,1)} %get-tuple-element.32), calls=%async_computation.1 | async-start | bytes 2359296 | tf_op jit(solution)/shard_map/all_to_all | solution.py:62
  93.1 3.0 %broadcast_in_dim.67 = f32[384,64,64]{0,2,1:T(8,128)} broadcast(f32[384,64]{0,1:T(8,128)S(1)} %get-tuple-element.67), dimensions={0,1} | broadcast | bytes 6389760 | tf_op jit(solution)/shard_map/broadcast_in_dim | solution.py:27
  96.1 6.7 %copy.24 = f32[384,4096]{1,0:T(8,128)} copy(f32[384,4096]{0,1:T(8,128)} %bitcast.52) | data formatting | bytes 12582912 | tf_op jit(solution)/shard_map/reshape | solution.py:27
  102.8 19.9 %all-to-all-done.1 = bf16[16,144,256]{2,1,0:T(8,128)(2,1)S(1)} async-done(((bf16[16,144,256]{2,1,0:T(8,128)(2,1)}), bf16[16,144,256]{2,1,0:T(8,128)(2,1)S(1)}, u32[]{:S(2)}, u32[]{:S(2)}) %all-to-all-start.1) | async-done | bytes 1179680 | tf_op jit(solution)/shard_map/all_to_all | solution.py:62
  122.7 1.6 %copy.22 = bf16[16,144,256]{1,2,0:T(8,128)(2,1)S(1)} copy(bf16[16,144,256]{2,1,0:T(8,128)(2,1)S(1)} %all-to-all-done.1) | data formatting | bytes 2359296 | tf_op jit(solution)/shard_map/all_to_all | solution.py:62
  124.3 1.2 slice.63
  125.5 0.1 copy.27
  125.6 0.6 slice.62
  126.9 0.8 convert_compare_fusion
  127.6 4.8 %fusion.20 = f32[384,4096]{1,0:T(8,128)} fusion(bf16[128,4096]{0,1:T(8,128)(2,1)} %bitcast.56, pred[384]{0:T(512)(128)(4,1)S(1)} %convert_compare_fusion, bf16[384,256]{1,0:T(8,128)(2,1)S(1)} %copy-done.1), kind=kOutput, calls=%fused_computation.39 | convolution fusion | flops 402702336 | bytes 7438848 | tf_op jit(solution)/shard_map/dot_general | solution.py:66
  132.5 14.2 %multiply_reduce_fusion = (f32[384]{0:T(512)S(1)}, f32[384,4096]{1,0:T(8,128)}) fusion(bf16[384,4096]{1,0:T(8,128)(2,1)} %param.12, bf16[384,4096]{1,0:T(8,128)(2,1)} %param.11, f32[4096]{0:T(1024)S(1)} %mul.106, f32[384,4096]{1,0:T(8,128)} %copy.24, f32[384,4096]{1,0:T(8,128)} %fusion.20, f32[4096]{0:T(1024)S(1)} %mul.100, f32[384,4096]{1,0:T(8,128)} %copy.20, ...), kind=kOutput, calls=%fused_computation.25 | convolution fusion | flops 1276329600 | bytes 34838016 | tf_op jit(solution)/shard_map/dot_general | solution.py:67
  146.7 5.4 %multiply_convert_fusion = bf16[384,4096]{1,0:T(8,128)(2,1)} fusion(f32[384,4096]{1,0:T(8,128)} %get-tuple-element.74, f32[4096]{0:T(1024)S(1)} %copy-done.2, f32[384]{0:T(512)S(1)} %add_rsqrt_fusion), kind=kLoop, calls=%fused_computation.24 | loop fusion | flops 4718592 | bytes 9455104 | tf_op jit(solution)/shard_map/convert_element_type | solution.py:74
  (163 shorter events, 3.2 us)
Async XLA Ops:
  23.4 6.8 %copy-start = (bf16[384,4096]{1,0:T(8,128)(2,1)S(1)}, bf16[384,4096]{1,0:T(8,128)(2,1)}, u32[]{:S(2)}) copy-start(bf16[384,4096]{1,0:T(8,128)(2,1)} %param.11) | copy-start | bytes 9437188
  23.4 6.8 %copy-start.1 = (bf16[384,256]{1,0:T(8,128)(2,1)S(1)}, bf16[384,256]{1,0:T(8,128)(2,1)}, u32[]{:S(2)}) copy-start(bf16[384,256]{1,0:T(8,128)(2,1)} %param.13) | copy-start | bytes 589828
  39.8 34.2 %all-to-all-start = ((bf16[16,144,256]{2,1,0:T(8,128)(2,1)}), bf16[16,144,256]{2,1,0:T(8,128)(2,1)S(1)}, u32[]{:S(2)}, u32[]{:S(2)}) async-start(bf16[16,144,256]{2,1,0:T(8,128)(2,1)} %bitcast.11), calls=%async_computation | async-start | bytes 2359296 | tf_op jit(solution)/shard_map/all_to_all | solution.py:47
  89.2 33.4 %all-to-all-start.1 = ((bf16[16,144,256]{2,1,0:T(8,128)(2,1)}), bf16[16,144,256]{2,1,0:T(8,128)(2,1)S(1)}, u32[]{:S(2)}, u32[]{:S(2)}) async-start(bf16[16,144,256]{2,1,0:T(8,128)(2,1)} %get-tuple-element.32), calls=%async_computation.1 | async-start | bytes 2359296 | tf_op jit(solution)/shard_map/all_to_all | solution.py:62
  132.5 14.2 %copy-start.2 = (f32[4096]{0:T(1024)S(1)}, f32[4096]{0:T(1024)}, u32[]{:S(2)}) copy-start(f32[4096]{0:T(1024)} %param.19) | copy-start | bytes 49156
where the time goes:
time: 153 us; the launch traced here: 152 us
  waiting for transfers between devices  49.7 us (32%)
  local copies, waits for them, and re-layouts  31.9 us (21%)
  matrix products  24 us (16%)
  other arithmetic  22.5 us (15%)
  blocking collectives  13.5 us (9%)
  starting transfers between devices  8.15 us (5%)
    all_to_all x1, waiting for transfers between devices, shards(): lax.all_to_all(block, SPAN_AXES, split_axis=0, concat_axis=0, tiled=True)  29.8 us
    all_to_all x1, waiting for transfers between devices, shards(): lax.all_to_all(give, SPAN_AXES, split_axis=0, concat_axis=0, tiled=True)  19.9 us
    dot_general x1, matrix products, shards(): local = jnp.dot(scores, weighted, preferred_element_type=f32)  14.2 us
    all_gather x1, blocking collectives, shards(): lax.all_gather(jnp.stack([dt_bias, decay_rate, skip]), 'head', axis=1, ti...  13.5 us
    reshape x2, local copies, waits for them, and re-layouts, shards(): spread = lambda v: jnp.repeat(v, hdim, axis=-1)  13.4 us
    dynamic_update_slice x16, other arithmetic, shards(): lax.scan(advance, (jnp.zeros((STATE, own), f32), jnp.full((own,), -1.0, f...  11.6 us
    broadcast_in_dim x6, local copies, waits for them, and re-layouts, shards(): spread = lambda v: jnp.repeat(v, hdim, axis=-1)  6.4 us
    concatenate x2, local copies, waits for them, and re-layouts, shards(): block = jnp.concatenate([state, extra])  5.48 us
  transfers between devices with their start and end apart: 2, of which 2 were waited for; matrix products, arithmetic and copies ran while one was open for 6% of the time, Pallas kernels for 0%

commit v1 on v0

--- a/solution.py
+++ b/solution.py
@@ -8,6 +8,16 @@
 SPAN_AXES = ("ctx", "head")
 
 
+def collect(x, axis, dim):
+    ways, here, hop = (lax.axis_size(axis), lax.axis_index(axis), x.shape[dim])
+    shape = [n * ways if d == dim else n for d, n in enumerate(x.shape)]
+    full = lax.dynamic_update_slice_in_dim(jnp.zeros(shape, x.dtype), x, here * hop, axis=dim)
+    for far in range(1, ways):
+        x = lax.ppermute(x, axis, [(d, (d + 1) % ways) for d in range(ways)])
+        full = lax.dynamic_update_slice_in_dim(full, x, (here - far) % ways * hop, axis=dim)
+    return full
+
+
 def shards(xs, gate_in, bc, dt_raw, doc_ids, dt_bias, decay_rate, skip, norm_gain):
     f32, bf16 = (jnp.float32, jnp.bfloat16)
     tokens, columns = xs.shape
@@ -15,7 +25,7 @@
     hdim = columns // heads
     devices = lax.axis_size("ctx") * lax.axis_size("head")
     own = columns // devices
-    params = lax.all_gather(jnp.stack([dt_bias, decay_rate, skip]), "head", axis=1, tiled=True)
+    params = collect(jnp.stack([dt_bias, decay_rate, skip]), "head", 1)
     ids = lax.dynamic_slice(doc_ids, (lax.axis_index("head") * tokens,), (tokens,))
     dt = jax.nn.softplus(dt_raw.astype(f32) + params[0][None, :])
     lower = jnp.arange(tokens)[:, None] >= jnp.arange(tokens)[None, :]

time: 153 us -> 152 us (level)
  blocking collectives: 13.5 us -> 0 us
  waiting for transfers between devices: 49.7 us -> 58.7 us
  starting transfers between devices: 8.15 us -> 12 us
    all_gather x1 -> x0, blocking collectives: 13.5 us -> none  [shards(): lax.all_gather(jnp.stack([dt_bias, decay_rate, skip]), 'head', axis=1, ti...]
    ppermute x0 -> x3, waiting for transfers between devices: none -> 8.93 us  [collect(): x = lax.ppermute(x, axis, [(d, (d + 1) % ways) for d in range(ways)])]
    ppermute x0 -> x3, starting transfers between devices: none -> 4.55 us  [collect(): x = lax.ppermute(x, axis, [(d, (d + 1) % ways) for d in range(ways)])]
  transfers between devices with their start and end apart: 2 -> 5, of which waited for: 2 -> 5; matrix products, arithmetic and copies ran while one was open for 6% -> 9% of each run, Pallas kernels for 0% -> 0%
where the time goes in v1:
time: 152 us; the launch traced here: 151 us
  waiting for transfers between devices  58.7 us (39%)
  local copies, waits for them, and re-layouts  32.2 us (21%)
  matrix products  23.9 us (16%)
  other arithmetic  22.5 us (15%)
  starting transfers between devices  12 us (8%)
    all_to_all x1, waiting for transfers between devices, shards(): lax.all_to_all(block, SPAN_AXES, split_axis=0, concat_axis=0, tiled=True)  29.7 us
    all_to_all x1, waiting for transfers between devices, shards(): lax.all_to_all(give, SPAN_AXES, split_axis=0, concat_axis=0, tiled=True)  20 us
    dot_general x1, matrix products, shards(): local = jnp.dot(scores, weighted, preferred_element_type=f32)  14.1 us
    reshape x2, local copies, waits for them, and re-layouts, shards(): spread = lambda v: jnp.repeat(v, hdim, axis=-1)  13.3 us
    dynamic_update_slice x16, other arithmetic, shards(): lax.scan(advance, (jnp.zeros((STATE, own), f32), jnp.full((own,), -1.0, f...  11.6 us
    ppermute x3, waiting for transfers between devices, collect(): x = lax.ppermute(x, axis, [(d, (d + 1) % ways) for d in range(ways)])  8.93 us
    broadcast_in_dim x6, local copies, waits for them, and re-layouts, shards(): spread = lambda v: jnp.repeat(v, hdim, axis=-1)  6.38 us
    concatenate x2, local copies, waits for them, and re-layouts, shards(): block = jnp.concatenate([state, extra])  5.48 us
  transfers between devices with their start and end apart: 5, of which 5 were waited for; matrix products, arithmetic and copies ran while one was open for 9% of the time, Pallas kernels for 0%

profile of v1, /device:TPU:0, one launch (start us, length us, event | category | flops | bytes accessed | tf_op | source)
XLA Modules:
  0.0 151.5 jit_solution(5026727425285963729)
XLA Ops:
  0.0 0.7 pad_maximum_fusion
  0.7 3.1 %collective-permute-start = (f32[3,16]{1,0:T(4,128)S(1)}, f32[3,16]{1,0:T(4,128)S(1)}, u32[]{:S(2)}, u32[]{:S(2)}) collective-permute-start(f32[3,16]{1,0:T(4,128)S(1)} %pad_maximum_fusion), channel_id=1, source_target_pairs={{0,1},{1,2},{2,3},{3,0},{4,5},{5,6},{6,7},{7,4},{8,9},{9,10},{10,1... | collective-permute-start | bytes 584 | tf_op jit(solution)/shard_map/ppermute | solution.py:16
  3.8 0.8 dynamic_slice.7
  4.5 0.6 slice.52
  5.1 1.4 broadcast_compare_fusion
  7.3 1.5 collective-permute-start.1
  8.9 3.8 %collective-permute-done.1 = f32[3,16]{1,0:T(4,128)S(1)} collective-permute-done((f32[3,16]{1,0:T(4,128)S(1)}, f32[3,16]{1,0:T(4,128)S(1)}, u32[]{:S(2)}, u32[]{:S(2)}) %collective-permute-start.1) | collective-permute-done | bytes 224 | tf_op jit(solution)/shard_map/ppermute | solution.py:16
  12.7 0.2 dynamic_update_slice.17
  12.9 0.2 dynamic_update_slice.18
  13.1 5.0 %collective-permute-done.2 = f32[3,16]{1,0:T(4,128)S(1)} collective-permute-done((f32[3,16]{1,0:T(4,128)S(1)}, f32[3,16]{1,0:T(4,128)S(1)}, u32[]{:S(2)}, u32[]{:S(2)}) %collective-permute-start.2) | collective-permute-done | bytes 224 | tf_op jit(solution)/shard_map/ppermute | solution.py:16
  18.1 0.2 dynamic_update_slice.19
  18.3 1.3 convolution_negate_fusion
  19.6 0.2 exponential_reduce_fusion
  19.8 0.9 exponential_multiply_fusion
  20.9 3.1 %broadcast_in_dim.73 = f32[384,64,64]{0,2,1:T(8,128)} broadcast(f32[384,64]{0,1:T(8,128)S(1)} %get-tuple-element.66), dimensions={0,1} | broadcast | bytes 6389760 | tf_op jit(solution)/shard_map/broadcast_in_dim | solution.py:37
  24.0 6.7 %copy.18 = f32[384,4096]{1,0:T(8,128)} copy(f32[384,4096]{0,1:T(8,128)} %bitcast.44) | data formatting | bytes 12582912 | tf_op jit(solution)/shard_map/reshape | solution.py:37
  30.7 3.7 %fusion.12 = bf16[128,4096]{1,0:T(8,128)(2,1)S(1)} fusion(f32[4096]{0:T(1024)S(1)} %mul.116, pred[384]{0:T(512)(128)(4,1)S(1)} %broadcast_compare_fusion, bf16[384,256]{1,0:T(8,128)(2,1)S(1)} %copy-done.1, f32[384,4096]{1,0:T(8,128)} %copy.18, bf16[384,4096]{1,0:T(8,128)(2,1)S(1)} %copy-done), kind=kOutput, calls=%fused_computation.27 | convolution fusion | flops 408469504 | bytes 10600960 | tf_op jit(solution)/shard_map/sn,sq->nq/dot_general | solution.py:46
  34.9 5.4 %concatenate.10 = bf16[144,16,256]{2,0,1:T(8,128)(2,1)} concatenate(bf16[128,16,256]{2,0,1:T(8,128)(2,1)S(1)} %bitcast.48, bf16[1,16,256]{2,0,1:T(2,128)(2,1)S(1)} %get-tuple-element.69, bf16[1,16,256]{2,0,1:T(2,128)(2,1)S(1)} %get-tuple-element.68, bf16[1,16,256]{2,0,1:T(2,128)(2,1)S(1)} %stack_broadcast_in_dim.3, bf16[13,16,256]{2,0,1:T(8,128)(2,1)S(1)} %broadcast_in_dim.81), dimensions={0} | concatenate | bytes 2359296 | tf_op jit(solution)/shard_map/concatenate | solution.py:55
  40.3 3.7 %all-to-all-start = ((bf16[16,144,256]{2,1,0:T(8,128)(2,1)}), bf16[16,144,256]{2,1,0:T(8,128)(2,1)S(1)}, u32[]{:S(2)}, u32[]{:S(2)}) async-start(bf16[16,144,256]{2,1,0:T(8,128)(2,1)} %bitcast.8), calls=%async_computation | async-start | bytes 2359296 | tf_op jit(solution)/shard_map/all_to_all | solution.py:57
  44.0 29.7 %all-to-all-done = bf16[16,144,256]{2,1,0:T(8,128)(2,1)S(1)} async-done(((bf16[16,144,256]{2,1,0:T(8,128)(2,1)}), bf16[16,144,256]{2,1,0:T(8,128)(2,1)S(1)}, u32[]{:S(2)}, u32[]{:S(2)}) %all-to-all-start) | async-done | bytes 1179680 | tf_op jit(solution)/shard_map/all_to_all | solution.py:57
  73.7 15.2 %while.15 = (s32[]{:T(128)}, f32[128,256]{1,0:T(8,128)S(1)}, f32[256]{0:T(256)S(1)}, bf16[16,144,256]{2,1,0:T(8,128)(2,1)}, bf16[16,144,256]{2,1,0:T(8,128)(2,1)...) while((s32[]{:T(128)}, f32[128,256]{1,0:T(8,128)S(1)}, ...), condition=%wide.region_1.2_spmd.clone, body=%wide.region_0.1_spmd.clone.sunk | while | flops 386822 | bytes 677192 | solution.py:69
  74.0 0.7 fusion.57
  74.9 0.7 fusion.57
  75.9 0.7 fusion.57
  76.8 0.7 fusion.57
  77.8 0.7 fusion.57
  78.7 0.7 fusion.57
  79.7 0.7 fusion.57
  80.6 0.7 fusion.57
  81.6 0.7 fusion.57
  82.5 0.7 fusion.57
  83.5 0.7 fusion.57
  84.4 0.7 fusion.57
  85.4 0.7 fusion.57
  86.3 0.7 fusion.57
  87.3 0.7 fusion.57
  88.2 0.7 fusion.57
  89.0 3.7 %all-to-all-start.1 = ((bf16[16,144,256]{2,1,0:T(8,128)(2,1)}), bf16[16,144,256]{2,1,0:T(8,128)(2,1)S(1)}, u32[]{:S(2)}, u32[]{:S(2)}) async-start(bf16[16,144,256]{2,1,0:T(8,128)(2,1)} %get-tuple-element.32), calls=%async_computation.1 | async-start | bytes 2359296 | tf_op jit(solution)/shard_map/all_to_all | solution.py:72
  92.8 3.0 %broadcast_in_dim.71 = f32[384,64,64]{0,2,1:T(8,128)} broadcast(f32[384,64]{0,1:T(8,128)S(1)} %get-tuple-element.67), dimensions={0,1} | broadcast | bytes 6389760 | tf_op jit(solution)/shard_map/broadcast_in_dim | solution.py:37
  95.8 6.5 %copy.22 = f32[384,4096]{1,0:T(8,128)} copy(f32[384,4096]{0,1:T(8,128)} %bitcast.45) | data formatting | bytes 12582912 | tf_op jit(solution)/shard_map/reshape | solution.py:37
  102.4 20.0 %all-to-all-done.1 = bf16[16,144,256]{2,1,0:T(8,128)(2,1)S(1)} async-done(((bf16[16,144,256]{2,1,0:T(8,128)(2,1)}), bf16[16,144,256]{2,1,0:T(8,128)(2,1)S(1)}, u32[]{:S(2)}, u32[]{:S(2)}) %all-to-all-start.1) | async-done | bytes 1179680 | tf_op jit(solution)/shard_map/all_to_all | solution.py:72
  122.4 1.6 %copy.20 = bf16[16,144,256]{1,2,0:T(8,128)(2,1)S(1)} copy(bf16[16,144,256]{2,1,0:T(8,128)(2,1)S(1)} %all-to-all-done.1) | data formatting | bytes 2359296 | tf_op jit(solution)/shard_map/all_to_all | solution.py:72
  124.0 1.2 slice.63
  125.3 0.5 slice.62
  126.3 0.8 convert_compare_fusion
  127.1 4.8 %fusion.20 = f32[384,4096]{1,0:T(8,128)} fusion(bf16[128,4096]{0,1:T(8,128)(2,1)} %bitcast.49, pred[384]{0:T(512)(128)(4,1)S(1)} %convert_compare_fusion, bf16[384,256]{1,0:T(8,128)(2,1)S(1)} %copy-done.1), kind=kOutput, calls=%fused_computation.39 | convolution fusion | flops 402702336 | bytes 7438848 | tf_op jit(solution)/shard_map/dot_general | solution.py:76
  132.0 14.1 %multiply_reduce_fusion = (f32[384]{0:T(512)S(1)}, f32[384,4096]{1,0:T(8,128)}) fusion(bf16[384,4096]{1,0:T(8,128)(2,1)} %param.12, bf16[384,4096]{1,0:T(8,128)(2,1)} %param.11, f32[4096]{0:T(1024)S(1)} %mul.122, f32[384,4096]{1,0:T(8,128)} %copy.22, f32[384,4096]{1,0:T(8,128)} %fusion.20, f32[4096]{0:T(1024)S(1)} %mul.116, f32[384,4096]{1,0:T(8,128)} %copy.18, ...), kind=kOutput, calls=%fused_computation.25 | convolution fusion | flops 1276329600 | bytes 34838016 | tf_op jit(solution)/shard_map/dot_general | solution.py:77
  146.0 5.4 %multiply_convert_fusion = bf16[384,4096]{1,0:T(8,128)(2,1)} fusion(f32[384,4096]{1,0:T(8,128)} %get-tuple-element.74, f32[4096]{0:T(1024)S(1)} %copy-done.2, f32[384]{0:T(512)S(1)} %add_rsqrt_fusion), kind=kLoop, calls=%fused_computation.24 | loop fusion | flops 4718592 | bytes 9455104 | tf_op jit(solution)/shard_map/convert_element_type | solution.py:84
  (171 shorter events, 3.9 us)
Async XLA Ops:
  0.7 6.7 %collective-permute-start = (f32[3,16]{1,0:T(4,128)S(1)}, f32[3,16]{1,0:T(4,128)S(1)}, u32[]{:S(2)}, u32[]{:S(2)}) collective-permute-start(f32[3,16]{1,0:T(4,128)S(1)} %pad_maximum_fusion), channel_id=1, source_target_pairs={{0,1},{1,2},{2,3},{3,0},{4,5},{5,6},{6,7},{7,4},{8,9},{9,10},{10,1... | collective-permute-start | bytes 584 | tf_op jit(solution)/shard_map/ppermute | solution.py:16
  7.3 5.4 %collective-permute-start.1 = (f32[3,16]{1,0:T(4,128)S(1)}, f32[3,16]{1,0:T(4,128)S(1)}, u32[]{:S(2)}, u32[]{:S(2)}) collective-permute-start(f32[3,16]{1,0:T(4,128)S(1)} %collective-permute-done), channel_id=1, source_target_pairs={{0,1},{1,2},{2,3},{3,0},{4,5},{5,6},{6,7},{7,4},{8,9},{9,10},{10,1... | collective-permute-start | bytes 584 | tf_op jit(solution)/shard_map/ppermute | solution.py:16
  12.7 5.4 %collective-permute-start.2 = (f32[3,16]{1,0:T(4,128)S(1)}, f32[3,16]{1,0:T(4,128)S(1)}, u32[]{:S(2)}, u32[]{:S(2)}) collective-permute-start(f32[3,16]{1,0:T(4,128)S(1)} %collective-permute-done.1), channel_id=1, source_target_pairs={{0,1},{1,2},{2,3},{3,0},{4,5},{5,6},{6,7},{7,4},{8,9},{9,10},{10,1... | collective-permute-start | bytes 584 | tf_op jit(solution)/shard_map/ppermute | solution.py:16
  24.0 6.7 %copy-start = (bf16[384,4096]{1,0:T(8,128)(2,1)S(1)}, bf16[384,4096]{1,0:T(8,128)(2,1)}, u32[]{:S(2)}) copy-start(bf16[384,4096]{1,0:T(8,128)(2,1)} %param.11) | copy-start | bytes 9437188
  24.0 6.7 %copy-start.1 = (bf16[384,256]{1,0:T(8,128)(2,1)S(1)}, bf16[384,256]{1,0:T(8,128)(2,1)}, u32[]{:S(2)}) copy-start(bf16[384,256]{1,0:T(8,128)(2,1)} %param.13) | copy-start | bytes 589828
  40.3 33.4 %all-to-all-start = ((bf16[16,144,256]{2,1,0:T(8,128)(2,1)}), bf16[16,144,256]{2,1,0:T(8,128)(2,1)S(1)}, u32[]{:S(2)}, u32[]{:S(2)}) async-start(bf16[16,144,256]{2,1,0:T(8,128)(2,1)} %bitcast.8), calls=%async_computation | async-start | bytes 2359296 | tf_op jit(solution)/shard_map/all_to_all | solution.py:57
  89.0 33.4 %all-to-all-start.1 = ((bf16[16,144,256]{2,1,0:T(8,128)(2,1)}), bf16[16,144,256]{2,1,0:T(8,128)(2,1)S(1)}, u32[]{:S(2)}, u32[]{:S(2)}) async-start(bf16[16,144,256]{2,1,0:T(8,128)(2,1)} %get-tuple-element.32), calls=%async_computation.1 | async-start | bytes 2359296 | tf_op jit(solution)/shard_map/all_to_all | solution.py:72
  132.0 14.1 %copy-start.2 = (f32[4096]{0:T(1024)S(1)}, f32[4096]{0:T(1024)}, u32[]{:S(2)}) copy-start(f32[4096]{0:T(1024)} %param.19) | copy-start | bytes 49156
